TPU v7x, 32 devices: a whole 2x2x4 slice. The times are simulated.
32 devices in a mesh: gx: 16 (over z, x, core), gz: 2 (over y).
Axes of the slice: x: 2, y: 2, z: 4, core: 2. Of those that a mesh axis runs over, the one named last changes fastest.
Arguments:
- velocity: float32 [8, 4, 2048, 512], P(None, None, 'gx', 'gz'), may hold values from -130 to 130
- kept: int32 [6], replicated, may hold values from 0 to 7, as said below
- shift: int32 [7], replicated, may hold values from 0 to 64, as said below
Outputs:
- correlation_map: float32 [7, 4, 2048, 512], P(None, None, 'gx', 'gz')
- coefficient: float32 [7, 4], replicated
Inputs may be any that keep to these rules, and one draw needn't show every extreme that they name: `kept`: 6 distinct snapshot indices in increasing order. `shift`: not falling with the separation; the shift of the longest separation is 64.
All inputs are finite; a program needn't handle non-finite values.
Results may differ from a plain program's by a relative error of at most 0.0001.
Values sent between devices are 32-bit elements; how exact they have to be, the bound alone decides.
A program may use at most 128 MiB of HBM per device.

v0:
```python
import math

import jax
import jax.numpy as jnp
from jax import lax
from jax.sharding import PartitionSpec as P

gauss_raw = [math.exp(-k * k / 8.0) for k in range(-4, 5)]
gauss_taps = [v / sum(gauss_raw) for v in gauss_raw]


def with_halo(cells, sides, width):
    for axis, dim in sides:
        count = lax.axis_size(axis)
        head = lax.slice_in_dim(cells, 0, width, axis=dim)
        tail = lax.slice_in_dim(cells, cells.shape[dim] - width, cells.shape[dim], axis=dim)
        cells = jnp.concatenate(
            [
                lax.ppermute(tail, axis, [(i, (i + 1) % count) for i in range(count)]),
                cells,
                lax.ppermute(head, axis, [((i + 1) % count, i) for i in range(count)]),
            ],
            axis=dim,
        )
    return cells


def passed_along(block, axis, distance):
    devices = range(lax.axis_size(axis))
    route = [((i - distance) % len(devices), i) for i in devices]
    return lax.ppermute(block, axis, route)


def pass_along(padded, dim):
    length = padded.shape[dim] - 8
    result = jnp.zeros(padded.shape[:dim] + (length,) + padded.shape[dim + 1 :], jnp.float32)
    for index in range(9):
        result = result + gauss_taps[index] * lax.slice_in_dim(
            padded, index, index + length, axis=dim
        )
    return result


def smooth(field):
    padded_x = with_halo(field, (("gx", 2),), 4)
    along_x = pass_along(padded_x, 2)
    padded_z = with_halo(along_x, (("gz", 3),), 4)
    return pass_along(padded_z, 3)


def on_device(velocity, kept, shift):
    count_snap = velocity.shape[0]
    rows_dev = velocity.shape[2]
    slots = jnp.arange(count_snap, dtype=jnp.int32)
    matches = kept[None, :] == slots[:, None]
    member = jnp.sum(matches.astype(jnp.float32), axis=1)
    filtered = smooth(velocity)
    local_energy = jnp.sum(filtered * filtered, axis=(2, 3))
    incoming = passed_along(filtered, "gx", -1)
    extended = jnp.concatenate([filtered, incoming], axis=2)
    total_energy = lax.psum(local_energy, ("gx", "gz"))
    cells = rows_dev * lax.axis_size("gx") * velocity.shape[3] * lax.axis_size("gz")
    rms = jnp.sqrt(total_energy / cells + 1e-06)
    scaled = extended / rms[:, :, None, None]
    maps = []
    for sep in range(1, count_snap):
        weights = member[: count_snap - sep] * member[sep:]
        count = jnp.maximum(jnp.sum(weights), 1.0)
        later = lax.dynamic_slice_in_dim(scaled[sep:], shift[sep - 1], rows_dev, axis=2)
        earlier = scaled[: count_snap - sep, :, :rows_dev]
        total = jnp.sum(weights[:, None, None, None] * earlier * later, axis=0)
        maps.append(total / count)
    correlation_map = jnp.stack(maps, axis=0)
    local_sums = jnp.sum(correlation_map, axis=(2, 3))
    coefficient = lax.psum(local_sums, ("gx", "gz")) / cells
    return (correlation_map, coefficient)


def solution(mesh):
    return jax.shard_map(
        on_device,
        mesh=mesh,
        in_specs=(P(None, None, "gx", "gz"), P(), P()),
        out_specs=(P(None, None, "gx", "gz"), P()),
        check_vma=False,
    )
```

profile of v0, /device:TPU:0, one launch (start us, length us, event | category | flops | bytes accessed | tf_op | source)
XLA Modules:
  0.0 250.3 jit_solution(1329984855601309085)
XLA Ops:
  0.6 1.1 fusion.66
  1.7 0.1 copy.35
  1.8 5.5 %collective-permute-start.1 = (f32[8,4,4,256]{3,0,2,1:T(8,128)S(1)}, f32[8,4,4,256]{3,0,2,1:T(8,128)S(1)}, u32[]{:S(2)}, u32[]{:S(2)}) collective-permute-start(f32[8,4,4,256]{3,0,2,1:T(8,128)S(1)} %copy.35), channel_id=1, source_target_pairs={{2,0},{4,2},{6,4},{8,6},{10,8},{12,10},{14,12},{16,14},{18,16},{20... | collective-permute-start | bytes 393224 | tf_op jit(solution)/shard_map/ppermute | solution.py:21
  7.3 0.1 copy.34
  7.4 0.1 collective-permute-start
  7.4 5.3 %copy.25 = f32[8,4,128,256]{2,0,3,1:T(8,128)} copy(f32[8,4,128,256]{3,2,1,0:T(8,128)} %param.3) | data formatting | bytes 8388608 | tf_op args[0]
  12.7 0.0 collective-permute-done.1
  12.7 2.7 %copy.29 = f32[8,4,4,256]{2,0,3,1:T(8,128)} copy(f32[8,4,4,256]{3,0,2,1:T(8,128)S(1)} %collective-permute-done.1) | data formatting | bytes 262144 | tf_op jit(solution)/shard_map/ppermute | solution.py:21
  15.4 0.0 collective-permute-done
  15.4 2.7 %copy.24 = f32[8,4,4,256]{2,0,3,1:T(8,128)} copy(f32[8,4,4,256]{3,0,2,1:T(8,128)S(1)} %collective-permute-done) | data formatting | bytes 262144 | tf_op jit(solution)/shard_map/ppermute | solution.py:19
  18.0 30.8 %fusion.23 = f32[8,4,128,256]{2,0,3,1:T(8,128)S(1)} fusion(f32[8,4,128,256]{2,0,3,1:T(8,128)} %copy.25, f32[8,4,4,256]{2,0,3,1:T(8,128)} %copy.29, f32[8,4,4,256]{2,0,3,1:T(8,128)} %copy.24), kind=kLoop, calls=%fused_computation.42 | loop fusion | flops 26214400 | bytes 8650752 | tf_op jit(solution)/shard_map/add | solution.py:38
  48.8 1.6 collective-permute-start.3
  50.4 0.5 collective-permute-start.2
  50.9 2.2 collective-permute-done.3
  53.2 1.5 collective-permute-done.2
  54.7 9.0 %multiply_reduce_fusion = (f32[8,4]{0,1:T(4,128)S(1)}, f32[8,4,128,256]{2,0,3,1:T(8,128)}) fusion(f32[8,4,128,4]{2,0,3,1:T(8,128)S(1)} %collective-permute-done.3, f32[8,4,128,256]{2,0,3,1:T(8,128)S(1)} %fusion.23, f32[8,4,128,4]{2,0,3,1:T(8,128)S(1)} %collective-permute-done.2), kind=kLoop, calls=%fused_computation.78 | loop fusion | flops 28311520 | bytes 8519808 | tf_op jit(solution)/shard_map/reduce_sum | solution.py:58
  63.7 3.0 %collective-permute-start.4 = (f32[8,4,128,256]{2,0,3,1:T(8,128)}, f32[8,4,128,256]{2,0,3,1:T(8,128)}, u32[]{:S(2)}, u32[]{:S(2)}) collective-permute-start(f32[8,4,128,256]{2,0,3,1:T(8,128)} %get-tuple-element.21), channel_id=1, source_target_pairs={{2,0},{4,2},{6,4},{8,6},{10,8},{12,10},{14,12},{16,14},{18,16},{20... | collective-permute-start | bytes 12582920 | tf_op jit(solution)/shard_map/ppermute | solution.py:31
  66.7 0.0 copy-done.4
  66.7 0.6 fusion.68
  75.8 0.0 copy-done.5
  75.8 0.1 convert_reduce_fusion
  75.9 0.7 fusion.63
  77.3 0.7 fusion.62
  78.7 0.7 fusion.61
  80.1 0.7 fusion.60
  81.6 0.7 fusion.59
  83.0 0.7 fusion.58
  84.4 0.6 fusion.67
  90.6 57.4 %psum.14 = f32[8,4]{0,1:T(4,128)S(1)} all-reduce(f32[8,4]{0,1:T(4,128)S(1)} %get-tuple-element.20), channel_id=1, replica_groups=mesh['gx'=16,'gz'=2] {'gx','gz'}, use_global_device_ids=true, to_apply=%region_2.0 | all-reduce | flops 32 | bytes 256 | tf_op jit(solution)/shard_map/psum | solution.py:61
  147.9 0.0 collective-permute-done.4
  148.0 4.1 %maximum_divide_fusion = f32[8,4,256,256]{2,0,3,1:T(8,128)S(1)} fusion(f32[8,4,128,256]{2,0,3,1:T(8,128)} %collective-permute-done.4, f32[8,4,128,256]{2,0,3,1:T(8,128)} %get-tuple-element.21, f32[8,4]{0,1:T(4,128)S(1)} %add_sqrt_fusion), kind=kLoop, calls=%fused_computation.12 | loop fusion | flops 4194304 | bytes 16777344 | tf_op jit(solution)/shard_map/div | solution.py:64
  152.0 3.9 %slice.263 = f32[7,4,256,256]{2,0,3,1:T(8,128)} slice(f32[8,4,256,256]{2,0,3,1:T(8,128)S(1)} %maximum_divide_fusion), slice={[1:8], [0:4], [0:256], [0:256]} | slice | bytes 14680064 | tf_op jit(solution)/shard_map/slice | solution.py:69
  155.9 3.9 %slice.265 = f32[6,4,256,256]{2,0,3,1:T(8,128)} slice(f32[8,4,256,256]{2,0,3,1:T(8,128)S(1)} %maximum_divide_fusion), slice={[2:8], [0:4], [0:256], [0:256]} | slice | bytes 12582912 | tf_op jit(solution)/shard_map/slice | solution.py:69
  159.9 0.9 slice.267
  160.8 2.8 %slice.269 = f32[4,4,256,256]{2,0,3,1:T(4,128)} slice(f32[8,4,256,256]{2,0,3,1:T(8,128)S(1)} %maximum_divide_fusion), slice={[4:8], [0:4], [0:256], [0:256]} | slice | bytes 8388608 | tf_op jit(solution)/shard_map/slice | solution.py:69
  163.6 0.9 slice.271
  164.5 2.2 slice.273
  166.7 0.9 slice.275
  167.6 5.0 %fusion.45 = f32[4,128,256]{1,2,0:T(8,128)S(1)} fusion(f32[8,4,256,256]{2,0,3,1:T(8,128)S(1)} %maximum_divide_fusion, f32[7,4,256,256]{2,0,3,1:T(8,128)} %slice.263, s32[]{:T(128)S(6)} %select_n.21, f32[7]{0:T(128)S(1)} %get-tuple-element.19), kind=kLoop, calls=%fused_computation.67 | loop fusion | flops 2621440 | bytes 7864352 | tf_op jit(solution)/shard_map/reduce_sum | solution.py:71
  172.7 0.9 broadcast_divide_fusion.5
  173.5 5.0 %fusion.43 = f32[4,128,256]{1,2,0:T(8,128)S(1)} fusion(f32[8,4,256,256]{2,0,3,1:T(8,128)S(1)} %maximum_divide_fusion, f32[6,4,256,256]{2,0,3,1:T(8,128)} %slice.265, s32[]{:T(128)S(6)} %select_n.22, f32[6]{0:T(128)S(1)} %get-tuple-element.17), kind=kLoop, calls=%fused_computation.64 | loop fusion | flops 2228224 | bytes 6815772 | tf_op jit(solution)/shard_map/reduce_sum | solution.py:71
  178.5 0.9 broadcast_divide_fusion.4
  179.5 1.6 fusion.41
  181.0 0.8 broadcast_divide_fusion.3
  181.9 4.1 %fusion.53 = f32[4,128,256]{1,2,0:T(8,128)S(1)} fusion(f32[8,4,256,256]{2,0,3,1:T(8,128)S(1)} %maximum_divide_fusion, f32[4,4,256,256]{2,0,3,1:T(4,128)} %slice.269, s32[]{:T(128)S(6)} %select_n.24, f32[4]{0:T(128)S(1)} %get-tuple-element.13), kind=kLoop, calls=%fused_computation.84 | loop fusion | flops 1441792 | bytes 4718612 | tf_op jit(solution)/shard_map/reduce_sum | solution.py:71
  186.0 0.0 copy-start
  186.0 0.8 broadcast_divide_fusion.2
  186.9 1.6 fusion.51
  188.5 0.0 copy-start.1
  188.5 0.0 copy-start.2
  188.5 0.9 broadcast_divide_fusion.1
  189.4 0.0 copy-done
  189.4 1.6 fusion.55
  191.0 0.8 broadcast_divide_fusion
  191.9 1.1 fusion.57
  193.0 0.0 copy-done.1
  193.0 0.0 copy-done.2
  193.0 0.0 copy-done.3
  193.1 10.9 %stack.2 = f32[7,4,128,256]{2,0,3,1:T(8,128)} concatenate(f32[1,4,128,256]{2,0,3,1:T(1,128)S(1)} %bitcast.14, f32[1,4,128,256]{2,0,3,1:T(1,128)S(1)} %bitcast.15, f32[1,4,128,256]{2,0,3,1:T(1,128)S(1)} %bitcast.16, f32[1,4,128,256]{2,0,3,1:T(1,128)} %bitcast.17, f32[1,4,128,256]{2,0,3,1:T(1,128)} %bitcast.18, f32[1,4,128,256]{2,0,3,1:T(1,128)} %bitcast.19, ...), dimensions={0} | concatenate | bytes 7340032 | tf_op jit(solution)/shard_map/stack | solution.py:73
  204.0 2.6 %reduce_sum.157 = f32[7,4]{0,1:T(4,128)S(1)} reduce(f32[7,4,128,256]{2,0,3,1:T(8,128)} %stack.2, f32[]{:T(128)} %constant.11.clone.1), dimensions={2,3}, to_apply=%region_15.0 | reduce | flops 917476 | bytes 3670132 | tf_op jit(solution)/shard_map/reduce_sum | solution.py:74
  206.6 0.1 copy.33
  206.7 5.0 %copy.31 = f32[7,4,128,256]{3,2,1,0:T(8,128)} copy(f32[7,4,128,256]{2,0,3,1:T(8,128)} %stack.2) | data formatting | bytes 7340032
  211.7 38.0 %psum.15 = f32[7,4]{1,0:T(8,128)S(1)} all-reduce(f32[7,4]{1,0:T(8,128)S(1)} %copy.33), channel_id=1, replica_groups=mesh['gx'=16,'gz'=2] {'gx','gz'}, use_global_device_ids=true, to_apply=%region_16.0 | all-reduce | flops 28 | bytes 224 | tf_op jit(solution)/shard_map/psum | solution.py:75
  249.7 0.7 copy.32
  (6 shorter events, 0.0 us)
Async XLA Ops:
  1.8 10.9 %collective-permute-start.1 = (f32[8,4,4,256]{3,0,2,1:T(8,128)S(1)}, f32[8,4,4,256]{3,0,2,1:T(8,128)S(1)}, u32[]{:S(2)}, u32[]{:S(2)}) collective-permute-start(f32[8,4,4,256]{3,0,2,1:T(8,128)S(1)} %copy.35), channel_id=1, source_target_pairs={{2,0},{4,2},{6,4},{8,6},{10,8},{12,10},{14,12},{16,14},{18,16},{20... | collective-permute-start | bytes 393224 | tf_op jit(solution)/shard_map/ppermute | solution.py:21
  7.4 8.0 %collective-permute-start = (f32[8,4,4,256]{3,0,2,1:T(8,128)S(1)}, f32[8,4,4,256]{3,0,2,1:T(8,128)S(1)}, u32[]{:S(2)}, u32[]{:S(2)}) collective-permute-start(f32[8,4,4,256]{3,0,2,1:T(8,128)S(1)} %copy.34), channel_id=1, source_target_pairs={{0,2},{2,4},{4,6},{6,8},{8,10},{10,12},{12,14},{14,16},{16,18},{18... | collective-permute-start | bytes 393224 | tf_op jit(solution)/shard_map/ppermute | solution.py:19
  48.8 4.3 %collective-permute-start.3 = (f32[8,4,128,4]{2,0,3,1:T(8,128)S(1)}, f32[8,4,128,4]{2,0,3,1:T(8,128)S(1)}, u32[]{:S(2)}, u32[]{:S(2)}) collective-permute-start(f32[8,4,128,4]{2,0,3,1:T(8,128)S(1)} %get-tuple-element.23), channel_id=1, source_target_pairs={{1,0},{0,1},{3,2},{2,3},{5,4},{4,5},{7,6},{6,7},{9,8},{8,9},{11,10... | collective-permute-start | bytes 196616 | tf_op jit(solution)/shard_map/ppermute | solution.py:21
  50.4 16.3 %copy-start.4 = (s32[7]{0:T(128)S(1)}, s32[7]{0:T(128)}, u32[]{:S(2)}) copy-start(s32[7]{0:T(128)} %param.5) | copy-start | bytes 88
  50.4 25.3 %copy-start.5 = (s32[6]{0:T(128)S(1)}, s32[6]{0:T(128)}, u32[]{:S(2)}) copy-start(s32[6]{0:T(128)} %param.4) | copy-start | bytes 76
  50.4 4.3 %collective-permute-start.2 = (f32[8,4,128,4]{2,0,3,1:T(8,128)S(1)}, f32[8,4,128,4]{2,0,3,1:T(8,128)S(1)}, u32[]{:S(2)}, u32[]{:S(2)}) collective-permute-start(f32[8,4,128,4]{2,0,3,1:T(8,128)S(1)} %get-tuple-element.22), channel_id=1, source_target_pairs={{0,1},{1,0},{2,3},{3,2},{4,5},{5,4},{6,7},{7,6},{8,9},{9,8},{10,11... | collective-permute-start | bytes 196616 | tf_op jit(solution)/shard_map/ppermute | solution.py:19
  63.7 84.3 %collective-permute-start.4 = (f32[8,4,128,256]{2,0,3,1:T(8,128)}, f32[8,4,128,256]{2,0,3,1:T(8,128)}, u32[]{:S(2)}, u32[]{:S(2)}) collective-permute-start(f32[8,4,128,256]{2,0,3,1:T(8,128)} %get-tuple-element.21), channel_id=1, source_target_pairs={{2,0},{4,2},{6,4},{8,6},{10,8},{12,10},{14,12},{16,14},{18,16},{20... | collective-permute-start | bytes 12582920 | tf_op jit(solution)/shard_map/ppermute | solution.py:31
  186.0 3.4 %copy-start = (f32[2,4,256,256]{2,0,3,1:T(2,128)S(1)}, f32[2,4,256,256]{2,0,3,1:T(2,128)}, u32[]{:S(2)}) copy-start(f32[2,4,256,256]{2,0,3,1:T(2,128)} %slice.273) | copy-start | bytes 6291460
  188.5 4.5 %copy-start.1 = (f32[4,128,256]{1,2,0:T(8,128)S(1)}, f32[4,128,256]{1,2,0:T(8,128)}, u32[]{:S(2)}) copy-start(f32[4,128,256]{1,2,0:T(8,128)} %broadcast_divide_fusion.5) | copy-start | bytes 1572868
  188.5 4.5 %copy-start.2 = (f32[4,128,256]{1,2,0:T(8,128)S(1)}, f32[4,128,256]{1,2,0:T(8,128)}, u32[]{:S(2)}) copy-start(f32[4,128,256]{1,2,0:T(8,128)} %broadcast_divide_fusion.4) | copy-start | bytes 1572868
  188.5 4.5 %copy-start.3 = (f32[4,128,256]{1,2,0:T(8,128)S(1)}, f32[4,128,256]{1,2,0:T(8,128)}, u32[]{:S(2)}) copy-start(f32[4,128,256]{1,2,0:T(8,128)} %broadcast_divide_fusion.3) | copy-start | bytes 1572868
where the time goes:
time: 253 us; the launch traced here: 250 us
  blocking collectives  95.3 us (38%)
  other arithmetic  76.3 us (30%)
  local copies, waits for them, and re-layouts  45.4 us (18%)
  between operations  18.9 us (7%)
  starting transfers between devices  10.6 us (4%)
  waiting for transfers between devices  3.77 us (1%)
    psum x1, blocking collectives, on_device(): total_energy = lax.psum(local_energy, ('gx', 'gz'))  57.4 us
    psum x1, blocking collectives, on_device(): coefficient = lax.psum(local_sums, ('gx', 'gz')) / cells  38 us
    add x1, other arithmetic, pass_along(): result + gauss_taps[index] * lax.slice_in_dim(padded, index, index + leng...  30.8 us
    reduce_sum x6, other arithmetic, on_device(): total = jnp.sum(weights[:, None, None, None] * earlier * later, axis=0)  19 us
    slice x7, local copies, waits for them, and re-layouts, on_device(): scaled[sep:]  15.6 us
    unnamed x18, local copies, waits for them, and re-layouts  11.2 us
    another operation x1, local copies, waits for them, and re-layouts, on_device(): correlation_map = jnp.stack(maps, axis=0)  10.9 us
    reduce_sum x1, other arithmetic, on_device(): local_energy = jnp.sum(filtered * filtered, axis=(2, 3))  9 us
  transfers between devices with their start and end apart: 5, of which 2 were waited for; matrix products, arithmetic and copies ran while one was open for 6% of the time, Pallas kernels for 0%

commit v1 on v0

v1 whole, which is shorter than its diff:
```python
import functools
import math

import jax
import jax.numpy as jnp
from jax import lax
from jax.experimental import pallas as pl
from jax.experimental.pallas import tpu as pltpu
from jax.sharding import PartitionSpec as P

gauss_raw = [math.exp(-k * k / 8.0) for k in range(-4, 5)]
gauss_taps = [v / sum(gauss_raw) for v in gauss_raw]
MESH = pl.DeviceIdType.MESH
LANES = 128
REACH = 8
f32 = jnp.float32
bf16 = jnp.bfloat16


def tap_of(distance):
    value = jnp.zeros(distance.shape, f32)
    for k in range(5):
        value = jnp.where(distance == k, gauss_taps[4 + k], value)
    return value


def halves(x):
    hi = x.astype(bf16)
    return hi, (x - hi.astype(f32)).astype(bf16)


def remote(src_ref, dst_ref, send, recv, dev):
    return pltpu.make_async_remote_copy(
        src_ref=src_ref, dst_ref=dst_ref, send_sem=send, recv_sem=recv,
        device_id=dev, device_id_type=MESH)


def summed(tile, zbuf, xbuf, rz_send, rz_recv, rx_send, rx_recv):
    gx, gz = lax.axis_index("gx"), lax.axis_index("gz")
    nx, nz = lax.axis_size("gx"), lax.axis_size("gz")
    zbuf[gz] = tile

    def z_copy(k, send):
        k = k if send else nz - k
        who = lax.rem(gz + k, nz)
        at = gz if send else who
        sem = k if send else nz - k
        return remote(zbuf.at[at], zbuf.at[at], rz_send.at[sem], rz_recv.at[sem], (gx, who))

    @pl.loop(1, nz)
    def _(k):
        z_copy(k, True).start()

    @pl.loop(1, nz)
    def _(k):
        z_copy(k, False).wait_recv()

    xbuf[gx] = jnp.sum(zbuf[...], axis=0)

    def x_copy(k, send):
        k = k if send else nx - k
        who = lax.rem(gx + k, nx)
        at = gx if send else who
        sem = k if send else nx - k
        return remote(xbuf.at[at], xbuf.at[at], rx_send.at[sem], rx_recv.at[sem], (who, gz))

    @pl.loop(1, nx)
    def _(k):
        x_copy(k, True).start()

    @pl.loop(1, nx)
    def _(k):
        x_copy(k, False).wait_recv()

    result = jnp.sum(xbuf[...], axis=0)

    @pl.loop(1, nz)
    def _(k):
        z_copy(k, True).wait_send()

    @pl.loop(1, nx)
    def _(k):
        x_copy(k, True).wait_send()

    return result


def taps_x(zb, c, at, size):
    y = gauss_taps[4] * zb[c, at : at + size, :]
    for k in range(1, 5):
        y = y + gauss_taps[4 + k] * (zb[c, at - k : at - k + size, :] + zb[c, at + k : at + k + size, :])
    return y


def exchange(tiles, cells, vel_hbm, kept, shift, fb_hbm, tail_hbm, zx_hbm, inv, vel, fb, tail, zx, hx,
             head_s, head_r, main_s, main_r, up_s, up_r, edge, zh, whi, wlo, zb, eb,
             ez, ex, vel_sem, out_sem, x_send, x_recv, m_send, m_recv, z_send, z_recv,
             rz_send, rz_recv, rx_send, rx_recv):
    snaps, planes, deep, _, cols = vel.shape
    rows = 8 * deep
    nk = kept.shape[0]
    nx, nz = lax.axis_size("gx"), lax.axis_size("gz")
    gx, gz = lax.axis_index("gx"), lax.axis_index("gz")
    xp, xm = lax.rem(gx + 1, nx), lax.rem(gx + nx - 1, nx)
    zp, zm = lax.rem(gz + 1, nz), lax.rem(gz + nz - 1, nz)

    barrier = pltpu.get_barrier_semaphore()

    def greet(dev):
        pl.semaphore_signal(barrier, inc=1, device_id=dev, device_id_type=MESH)

    for dev in ((xm, zm), (xm, zp), (xp, zm), (xp, zp)):
        greet(dev)

    @pl.loop(1, nx)
    def _(k):
        greet((lax.rem(gx + k, nx), gz))

    @pl.loop(1, nz)
    def _(k):
        greet((gx, lax.rem(gz + k, nz)))

    loads = [pltpu.make_async_copy(vel_hbm.at[t], vel.at[t], vel_sem.at[t]) for t in range(snaps)]
    for c in loads:
        c.start()

    src = lax.broadcasted_iota(jnp.int32, (cols + 2 * LANES, cols), 0)
    dst = lax.broadcasted_iota(jnp.int32, (cols + 2 * LANES, cols), 1)
    place = jnp.where(src < cols, src, jnp.where(src < cols + LANES, src % 4 - 4, cols + src % 4))
    weights = tap_of(jnp.abs(place - dst))
    hi, lo = halves(weights)
    whi[...] = hi
    wlo[...] = lo

    reach = []
    start = []
    total = jnp.int32(0)
    for j in range(1, nk):
        s = shift[jnp.clip(kept[j] - kept[0] - 1, 0, snaps - 2)]
        n = (s + 3) // 8
        start.append(total)
        reach.append(n)
        total = total + n

    def source(m):
        j = jnp.int32(1)
        base = start[0]
        for i in range(2, nk):
            later = m >= start[i - 1]
            j = jnp.where(later, i, j)
            base = jnp.where(later, start[i - 1], base)
        return j, jnp.clip(m - base + 1, 1, REACH)

    for c in loads:
        c.wait()

    low = lax.broadcasted_iota(jnp.int32, (8, cols), 0) < 4

    @pl.loop(0, nk)
    def _(j):
        t = kept[j]
        for p in range(planes):
            head_s[j * planes + p] = vel[t, p, 0]
        for p in range(0, planes, 2):
            even = vel[t, p, deep - 1]
            odd = vel[t, p + 1, deep - 1]
            up_s[j * (planes // 2) + p // 2] = jnp.where(low, pltpu.roll(even, 4, 0), odd)

    pl.semaphore_wait(barrier, nx - 1 + nz - 1 + 4)

    head = remote(head_s, head_r, x_send.at[0], x_recv.at[0], (xm, gz))
    head.start()
    upper = remote(up_s, up_r, x_send.at[1], x_recv.at[1], (xp, gz))
    upper.start()

    @pl.loop(0, tiles)
    def _(m):
        j, q = source(m)
        t = kept[j]
        for p in range(planes):
            main_s[p, m] = vel[t, p, q]

    mains = [remote(main_s.at[p], main_r.at[p], m_send.at[p], m_recv.at[p], (xm, gz)) for p in range(planes)]
    mains[0].start()

    lane = lax.broadcasted_iota(jnp.int32, (rows, LANES), 1)
    edge[...] = jnp.zeros(edge.shape, f32)

    @pl.loop(0, nk)
    def _(j):
        t = kept[j]
        left, right = edge[0].reshape(rows, LANES), edge[1].reshape(rows, LANES)
        for p in range(planes):
            m = j * planes + p
            mine = lane // 4 == m
            block = vel[t, p].reshape(rows, cols)
            left = jnp.where(mine, pltpu.roll(block[:, :LANES], 4 * m, 1), left)
            right = jnp.where(mine, pltpu.roll(block[:, cols - LANES :], 4 * m + 4, 1), right)
        edge[0] = left.reshape(deep, 8, LANES)
        edge[1] = right.reshape(deep, 8, LANES)

    zs = []
    for side, (e, dz) in enumerate(((1, zp), (0, zm))):
        for n, (dx, a, size, at) in enumerate(((gx, 0, deep, 1), (xm, 0, REACH + 1, 1 + deep), (xp, deep - 1, 1, 0))):
            zs.append(remote(edge.at[e, pl.ds(a, size)], zh.at[side, pl.ds(at, size)],
                             z_send.at[3 * side + n], z_recv.at[3 * side + n], (dx, dz)))
    for c in zs:
        c.start()
    for c in mains[1:]:
        c.start()

    def along_z(x, sides, mine):
        sides = [jnp.where(mine, side.reshape(x.shape[0], LANES), 0.0) for side in sides]
        a, b = halves(jnp.concatenate([x] + sides, axis=1))
        dot = functools.partial(jnp.dot, preferred_element_type=f32)
        return dot(a, whi[...]) + dot(b, whi[...]) + dot(a, wlo[...])

    def along_x(m, c, first, size):
        y = taps_x(zb, c, first + 8, size)
        fb[m, c, first : first + size, :] = y
        return y

    head.wait_recv()
    upper.wait_recv()
    for c in zs:
        c.wait_recv()

    @pl.loop(0, nk * planes)
    def _(m):
        j, p = m // planes, m % planes
        t = kept[j]
        tile = up_r[m // 2]
        tile = jnp.where(p % 2 == 1, tile, pltpu.roll(tile, 4, 0))
        x = jnp.concatenate([tile, vel[t, p].reshape(rows, cols), head_r[m]], axis=0)
        mine = lax.broadcasted_iota(jnp.int32, (rows + 16, LANES), 1) // 4 == m
        y = along_z(x, [zh[side, : deep + 2] for side in range(2)], mine)
        for c in range(cols // LANES):
            zb[c] = y[:, c * LANES : (c + 1) * LANES]
            tail[m, c] = y[rows:, c * LANES : (c + 1) * LANES]
        energy = jnp.zeros((1, LANES), f32)
        for c in range(cols // LANES):
            for first in range(0, rows, 64):
                y = along_x(m, c, first, 64)
                energy = energy + jnp.sum(y * y, axis=0, keepdims=True)
        eb[pl.ds(m, 1), :] = energy

    lane8 = lax.broadcasted_iota(jnp.int32, (8, LANES), 1)

    tile = jnp.zeros((8, LANES), f32)
    groups = nk * planes // 8
    for g in range(groups):
        part = jnp.sum(eb[8 * g : 8 * g + 8, :], axis=1, keepdims=True)
        tile = jnp.where(lane8 == g, part, tile)
    local = [pltpu.make_async_copy(fb, fb_hbm, out_sem.at[planes]),
             pltpu.make_async_copy(tail, tail_hbm, out_sem.at[planes + 1])]
    for c in local:
        c.start()
    tile = summed(tile, ez, ex, rz_send, rz_recv, rx_send, rx_recv)
    for g in range(groups):
        mean = jnp.sum(jnp.where(lane8 == g, tile, 0.0), axis=1, keepdims=True) / cells
        inv[8 * g : 8 * g + 8, :] = jnp.broadcast_to(1.0 / jnp.sqrt(mean + 1e-06), (8, LANES))

    @pl.loop(0, tiles)
    def _(m):
        j, q = source(m)
        mine = lane8 // (4 * planes) == j
        for side in range(2):
            hx[side, m] = jnp.where(mine, zh[side, deep + 1 + q], 0.0)

    mine = lax.broadcasted_iota(jnp.int32, (8 * tiles, LANES), 1) // 4 % planes
    for p in range(planes):
        mains[p].wait_recv()
        y = along_z(main_r[p].reshape(8 * tiles, cols), [hx[0], hx[1]], mine == p)
        for c in range(cols // LANES):
            zx[p, c] = y[:, c * LANES : (c + 1) * LANES].reshape(tiles, 8, LANES)
        local.append(pltpu.make_async_copy(zx.at[p], zx_hbm.at[p], out_sem.at[p]))
        local[-1].start()

    head.wait_send()
    upper.wait_send()
    for c in zs:
        c.wait_send()
    for c in mains:
        c.wait_send()
    for c in local:
        c.wait()


def correlate(tiles, kept, shift, fb, tail, zx, inv, out, csum, table, pairs, number, zb, gb):
    nk, _, halves_z, rows, _ = fb.shape
    lags = shift.shape[0]
    p = pl.program_id(0)
    planes = pl.num_programs(0)

    @pl.when(p == 0)
    def _():
        for d in range(lags):
            number[d] = 0
        for i in range(nk):
            for j in range(i + 1, nk):
                d = jnp.clip(kept[j] - kept[i] - 1, 0, lags - 1)
                pairs[d, number[d]] = 8 * i + j
                number[d] = number[d] + 1
        total = jnp.int32(0)
        for j in range(1, nk):
            n = (shift[jnp.clip(kept[j] - kept[0] - 1, 0, lags - 1)] + 3) // 8
            table[0, j] = total
            table[1, j] = n
            total = total + n

    for j in range(nk):
        scale = inv[pl.ds(j * planes + p, 1), :]
        for c in range(halves_z):
            gb[j, c, :rows, :] = fb[j, 0, c] * scale

    @pl.loop(1, nk)
    def _(j):
        scale = inv[pl.ds(j * planes + p, 1), :]
        for c in range(halves_z):
            zb[c, 0:16, :] = tail[j, 0, c]
            for q in range(1, REACH + 1):
                at = table[0, j] + jnp.clip(q, 1, jnp.maximum(table[1, j], 1)) - 1
                zb[c, 8 + 8 * q : 16 + 8 * q, :] = zx[0, c, jnp.minimum(at, tiles - 1)]
            gb[j, c, rows:, :] = taps_x(zb, c, 8, 8 * REACH) * scale

    for d in range(lags):
        n = number[d]
        s = shift[d]
        share = 1.0 / jnp.maximum(n, 1).astype(f32)
        part = jnp.zeros((8, LANES), f32)
        for c in range(halves_z):
            for first in range(0, rows, 64):
                def add(i, acc):
                    code = pairs[d, i]
                    a, b = code // 8, code % 8
                    return acc + gb[a, c, first : first + 64, :] * gb[b, c, pl.ds(first + s, 64), :]

                acc = lax.fori_loop(0, n, add, jnp.zeros((64, LANES), f32)) * share
                out[d, 0, first : first + 64, c * LANES : (c + 1) * LANES] = acc
                part = part + jnp.sum(acc.reshape(8, 8, LANES), axis=0)
        csum[0, d] = part
    csum[0, lags] = jnp.zeros((8, LANES), f32)


def means(cells, csum, coef, cz, cx, rz_send, rz_recv, rx_send, rx_recv):
    nx, nz = lax.axis_size("gx"), lax.axis_size("gz")
    gx, gz = lax.axis_index("gx"), lax.axis_index("gz")
    barrier = pltpu.get_barrier_semaphore()

    @pl.loop(1, nx)
    def _(k):
        pl.semaphore_signal(barrier, inc=1, device_id=(lax.rem(gx + k, nx), gz), device_id_type=MESH)

    @pl.loop(1, nz)
    def _(k):
        pl.semaphore_signal(barrier, inc=1, device_id=(gx, lax.rem(gz + k, nz)), device_id_type=MESH)

    lane8 = lax.broadcasted_iota(jnp.int32, (8, LANES), 1)
    tile = jnp.zeros((8, LANES), f32)
    for p in range(csum.shape[0]):
        part = jnp.sum(jnp.sum(csum[p], axis=1), axis=1, keepdims=True)
        tile = jnp.where(lane8 == p, part, tile)
    pl.semaphore_wait(barrier, nx - 1 + nz - 1)
    tile = summed(tile, cz, cx, rz_send, rz_recv, rx_send, rx_recv)
    coef[...] = tile[: coef.shape[0], : coef.shape[1]] / cells


def on_device(velocity, kept, shift):
    snaps, planes, rows, cols = velocity.shape
    nk = kept.shape[0]
    nx, nz = lax.axis_size("gx"), lax.axis_size("gz")
    cells = rows * nx * cols * nz
    tiles = (nk - 1) * REACH
    n = nk * planes
    deep = rows // 8
    wide = cols // LANES
    dma = pltpu.SemaphoreType.DMA
    vmem = pl.BlockSpec(memory_space=pltpu.VMEM)
    smem = pl.BlockSpec(memory_space=pltpu.SMEM)
    anywhere = pl.BlockSpec(memory_space=pl.ANY)
    shape = jax.ShapeDtypeStruct
    sums = [dma((nz,)), dma((nz,)), dma((nx,)), dma((nx,))]
    tiled = velocity.reshape(snaps, planes, deep, 8, cols)
    fb, tail, zx, inv = pl.pallas_call(
        functools.partial(exchange, tiles, cells),
        out_shape=(shape((n, wide, rows, LANES), f32), shape((n, wide, 16, LANES), f32),
                   shape((planes, wide, tiles, 8, LANES), f32), shape((n, LANES), f32)),
        in_specs=[anywhere, smem, smem],
        out_specs=(anywhere, anywhere, anywhere, vmem),
        scratch_shapes=[
            pltpu.VMEM((snaps, planes, deep, 8, cols), f32),
            pltpu.VMEM((n, wide, rows, LANES), f32),
            pltpu.VMEM((n, wide, 16, LANES), f32),
            pltpu.VMEM((planes, wide, tiles, 8, LANES), f32),
            pltpu.VMEM((2, tiles, 8, LANES), f32),
            pltpu.VMEM((n, 8, cols), f32),
            pltpu.VMEM((n, 8, cols), f32),
            pltpu.VMEM((planes, tiles, 8, cols), f32),
            pltpu.VMEM((planes, tiles, 8, cols), f32),
            pltpu.VMEM((n // 2, 8, cols), f32),
            pltpu.VMEM((n // 2, 8, cols), f32),
            pltpu.VMEM((2, deep, 8, LANES), f32),
            pltpu.VMEM((2, deep + REACH + 2, 8, LANES), f32),
            pltpu.VMEM((cols + 2 * LANES, cols), bf16),
            pltpu.VMEM((cols + 2 * LANES, cols), bf16),
            pltpu.VMEM((wide, rows + 16, LANES), f32),
            pltpu.VMEM((n, LANES), f32),
            pltpu.VMEM((nz, 8, LANES), f32),
            pltpu.VMEM((nx, 8, LANES), f32),
            dma((snaps,)), dma((planes + 2,)),
            dma((2,)), dma((2,)), dma((planes,)), dma((planes,)), dma((6,)), dma((6,)),
        ] + sums,
        compiler_params=pltpu.CompilerParams(
            collective_id=0, has_side_effects=True, vmem_limit_bytes=48 * 1024 * 1024),
    )(tiled, kept, shift)
    maps, csum = pl.pallas_call(
        functools.partial(correlate, tiles),
        grid=(planes,),
        out_shape=(shape((snaps - 1, planes, rows, cols), f32), shape((planes, 8, 8, LANES), f32)),
        in_specs=[smem, smem,
                  pl.BlockSpec((nk, 1, wide, rows, LANES), lambda p: (0, p, 0, 0, 0)),
                  pl.BlockSpec((nk, 1, wide, 16, LANES), lambda p: (0, p, 0, 0, 0)),
                  pl.BlockSpec((1, wide, tiles, 8, LANES), lambda p: (p, 0, 0, 0, 0)),
                  pl.BlockSpec((n, LANES), lambda p: (0, 0))],
        out_specs=(pl.BlockSpec((snaps - 1, 1, rows, cols), lambda p: (0, p, 0, 0)),
                   pl.BlockSpec((1, 8, 8, LANES), lambda p: (p, 0, 0, 0))),
        scratch_shapes=[
            pltpu.SMEM((2, 8), jnp.int32),
            pltpu.SMEM((8, 16), jnp.int32),
            pltpu.SMEM((8,), jnp.int32),
            pltpu.VMEM((wide, 16 + 8 * REACH, LANES), f32),
            pltpu.VMEM((nk, wide, rows + 8 * REACH, LANES), f32),
        ],
        compiler_params=pltpu.CompilerParams(vmem_limit_bytes=48 * 1024 * 1024),
    )(kept, shift, fb.reshape(nk, planes, wide, rows, LANES), tail.reshape(nk, planes, wide, 16, LANES), zx, inv)
    coefficient = pl.pallas_call(
        functools.partial(means, cells),
        out_shape=shape((snaps - 1, planes), f32),
        in_specs=[vmem],
        out_specs=vmem,
        scratch_shapes=[pltpu.VMEM((nz, 8, LANES), f32), pltpu.VMEM((nx, 8, LANES), f32)] + sums,
        compiler_params=pltpu.CompilerParams(collective_id=1, has_side_effects=True),
    )(csum)
    return maps, coefficient


def solution(mesh):
    return jax.shard_map(
        on_device,
        mesh=mesh,
        in_specs=(P(None, None, "gx", "gz"), P(), P()),
        out_specs=(P(None, None, "gx", "gz"), P()),
        check_vma=False,
    )
```

time: 253 us -> 72.3 us (0.29)
  blocking collectives: 95.3 us -> 0 us
  other arithmetic: 76.3 us -> 0 us
  Pallas kernels: 0 us -> 68.2 us
  local copies, waits for them, and re-layouts: 45.4 us -> 3.28 us
  between operations: 18.9 us -> 0.66 us
  starting transfers between devices: 10.6 us -> 0 us
  waiting for transfers between devices: 3.77 us -> 0 us
    psum x2 -> x0, blocking collectives: 95.3 us -> none  [the longest x1 57.4 us: on_device(): total_energy = lax.psum(local_energy, ('gx', 'gz'))]
    pallas_call x0 -> x3, Pallas kernels: none -> 68.2 us  [the longest x1 45.8 us: on_device(): pl.pallas_call(functools.partial(exchange, tiles, cells), out_shape=(shap...]
    reduce_sum x15 -> x0, other arithmetic: 35.1 us -> none  [the longest x6 19 us: on_device(): total = jnp.sum(weights[:, None, None, None] * earlier * later, axis=0)]
    add x1 -> x0, other arithmetic: 30.8 us -> none  [pass_along(): result + gauss_taps[index] * lax.slice_in_dim(padded, index, index + leng...]
    slice x11 -> x0, local copies, waits for them, and re-layouts: 18 us -> none  [the longest x7 15.6 us: on_device(): scaled[sep:]]
    another operation x1 -> x0, local copies, waits for them, and re-layouts: 10.9 us -> none  [on_device(): correlation_map = jnp.stack(maps, axis=0)]
    ppermute x5 -> x0, starting transfers between devices: 10.6 us -> none  [the longest x2 7.05 us: with_halo(): lax.ppermute(head, axis, [((i + 1) % count, i) for i in range(count)])]
    div x9 -> x0, other arithmetic: 10.4 us -> none  [the longest x7 6.33 us: on_device(): maps.append(total / count)]
  transfers between devices with their start and end apart: 5 -> 0, of which waited for: 2 -> 0; matrix products, arithmetic and copies ran while one was open for 6% -> 0% of each run, Pallas kernels for 0% -> 0%
where the time goes in v1:
time: 72.3 us; the launch traced here: 72.2 us
  Pallas kernels  68.2 us (94%)
  local copies, waits for them, and re-layouts  3.28 us (5%)
    pallas_call x1, Pallas kernels, on_device(): pl.pallas_call(functools.partial(exchange, tiles, cells), out_shape=(shap...  45.8 us
    pallas_call x1, Pallas kernels, on_device(): pl.pallas_call(functools.partial(means, cells), out_shape=shape((snaps -...  12 us
    pallas_call x1, Pallas kernels, on_device(): pl.pallas_call(functools.partial(correlate, tiles), grid=(planes,), out_s...  10.4 us
    unnamed x7, local copies, waits for them, and re-layouts  3.28 us

profile of v1, /device:TPU:0, one launch (start us, length us, event | category | flops | bytes accessed | tf_op | source)
XLA Modules:
  0.0 72.2 jit_solution(14647305829454528050)
XLA Ops:
  0.6 0.0 copy-start.1
  0.6 0.6 copy-done.1
  1.3 0.0 copy-start.2
  1.3 0.7 copy-done.2
  1.9 45.8 %shard_map.50 = (f32[24,2,128,128]{3,2,1,0:T(8,128)S(1)}, f32[24,2,16,128]{3,2,1,0:T(8,128)S(1)}, f32[4,2,40,8,128]{4,3,2,1,0:T(8,128)S(1)}, f32[24,128]{1,0:T(8,128)S(1)}) custom-call(f32[8,4,16,8,256]{4,3,2,1,0:T(8,128)} %bitcast.5, s32[6]{0:T(128)S(1)} %copy-done.1, s32[7]{0:T(128)S(1)} %copy-done.2), custom_call_target="tpu_custom_call" | custom-call | tf_op jit(solution)/shard_map/pallas_call | solution.py:384
  47.8 10.4 %shard_map.51 = (f32[7,4,128,256]{3,2,1,0:T(8,128)}, f32[4,8,8,128]{3,2,1,0:T(8,128)S(1)}) custom-call(s32[6]{0:T(128)S(1)} %copy-done.1, s32[7]{0:T(128)S(1)} %copy-done.2, f32[6,4,2,128,128]{4,3,2,1,0:T(8,128)S(1)} %bitcast.3, f32[6,4,2,16,128]{4,3,2,1,0:T(8,128)S(1)} %bitcast.4, f32[4,2,40,8,128]{4,3,2,1,0:T(8,128)S(1)} %get-tuple-element.10.zx, ...), custom_call_target="tpu_custom_call" | custom-call | tf_op jit(solution)/shard_map/pallas_call | solution.py:416
  58.2 0.0 copy-start
  58.2 0.6 copy-done
  58.9 12.0 %shard_map.52 = f32[7,4]{1,0:T(8,128)} custom-call(f32[4,8,8,128]{3,2,1,0:T(8,128)} %copy-done), custom_call_target="tpu_custom_call" | custom-call | tf_op jit(solution)/shard_map/pallas_call | solution.py:436
  70.8 1.3 %copy.5 = f32[7,4]{0,1:T(4,128)} copy(f32[7,4]{1,0:T(8,128)} %shard_map.52) | data formatting | bytes 224
Async XLA Ops:
  0.6 0.7 copy-start.1
  1.3 0.7 copy-start.2
  58.2 0.7 copy-start
